TPU v7x, 32 devices: a whole 2x2x4 slice. The times are simulated.
32 devices in a mesh: seg: 4 (over x, core), sec: 8 (over z, y).
Axes of the slice: x: 2, y: 2, z: 4, core: 2. Of those that a mesh axis runs over, the one named last changes fastest.
Arguments:
- wave: bfloat16 [4, 8, 256, 256], P('seg', 'sec'), may hold values from -21 to 21
- diag_energy: float32 [4, 8, 2, 256], P('seg'), may hold values from 0.5 to 4
- term_list: int32 [4, 768, 4], P('seg', 'sec'), may hold values from 0 to 15, as said below
- term_count: int32 [4, 8], P('seg', 'sec'), may hold values from 19 to 96, as said below
- term_coef: float32 [4, 768], P('seg', 'sec'), may hold values from -0.6 to 0.6
- edge_env: bfloat16 [4, 128, 256, 256], P('seg', 'sec'), may hold values from -0.375 to 0.375
- right_env: bfloat16 [4, 128, 256, 256], P('seg', 'sec'), may hold values from -0.375 to 0.375
Outputs:
- image0: float32 [4, 8, 256, 256], P('seg', 'sec')
- search: bfloat16 [4, 8, 256, 256], P('seg', 'sec')
- image1: float32 [4, 8, 256, 256], P('seg', 'sec')
Inputs may be any that keep to these rules, and one draw needn't show every extreme that they name: `term_list`: columns 0 and 1 name blocks of the segment, 0 to 7; column 2 names a channel held by the same device, 0 to 15; column 3 is 0 or 1. Rows at or past a device's count hold arbitrary values in these ranges. `term_count`: the live terms of a device are its first rows; in every segment one device holds exactly 96.
All inputs are finite; a program needn't handle non-finite values.
Results may differ from a plain program's by a relative error of at most 0.00115.
The roundings to bfloat16 on the way count: a program that leaves them out, or rounds other values in their place, can miss the bound.
Values may be sent and summed in bfloat16 or wider, within the bound.
A program may use at most 128 MiB of HBM per device.

v0:
```python
import functools

import jax
import jax.numpy as jnp
from jax import lax
from jax.experimental import pallas as pl
from jax.experimental.pallas import tpu as pltpu
from jax.sharding import PartitionSpec as P

STEP = 4
PARTS = 4
CUTS = 2
LEVELS = 32767.0
VM = pltpu.VMEM
SM = pltpu.SMEM


def shifted(value, axis, by):
    devices = lax.axis_size(axis)
    pairs = [(i, i + by) for i in range(devices) if 0 <= i + by < devices]
    return lax.ppermute(value, axis, pairs)


def partition(rows_ref, count_ref, coef_ref, packed_ref, weight_ref, many_ref):
    cap = packed_ref.shape[0] // 2

    def place(i, carry):
        n0, n1 = carry
        kind = rows_ref[3, i]
        at = jnp.where(kind == 1, cap + n1, n0)
        packed_ref[at] = rows_ref[0, i] + rows_ref[1, i] * 256 + rows_ref[2, i] * 65536
        weight_ref[at] = coef_ref[0, i]
        return n0 + 1 - kind, n1 + kind

    n0, n1 = lax.fori_loop(0, count_ref[0, 0], place, (jnp.int32(0), jnp.int32(0)))
    for extra in range(STEP):
        for at in (n0 + extra, cap + n1 + extra):
            packed_ref[at] = jnp.int32(0)
            weight_ref[at] = jnp.float32(0)
    many_ref[0] = n0
    many_ref[1] = n1


def fields(packed_ref, at):
    code = packed_ref[at]
    return code % 256, (code // 256) % 256, code // 65536


def add_plain(many, x_ref, right_ref, packed_ref, weight_ref, out_ref):
    def advance(turn, carry):
        done = []
        for u in range(STEP):
            at = turn * STEP + u
            src, tgt, chan = fields(packed_ref, at)
            product = jnp.dot(x_ref[src], right_ref[chan], preferred_element_type=jnp.float32)
            done.append((tgt, weight_ref[at], product))
        for tgt, weight, product in done:
            out_ref[tgt] += weight * product
        return carry

    lax.fori_loop(0, (many + STEP - 1) // STEP, advance, 0)


def add_left(many, x_ref, right_ref, left_ref, packed_ref, weight_ref, out_ref):
    cap = packed_ref.shape[0] // 2

    def advance(turn, carry):
        rounded = []
        for u in range(STEP):
            at = cap + turn * STEP + u
            src, tgt, chan = fields(packed_ref, at)
            product = jnp.dot(x_ref[src], right_ref[chan], preferred_element_type=jnp.float32)
            rounded.append((at, tgt, chan, product.astype(jnp.bfloat16)))
        done = []
        for at, tgt, chan, value in rounded:
            leftward = jnp.dot(left_ref[chan], value, preferred_element_type=jnp.float32)
            done.append((tgt, weight_ref[at], leftward))
        for tgt, weight, leftward in done:
            out_ref[tgt] += weight * leftward
        return carry

    lax.fori_loop(0, (many + STEP - 1) // STEP, advance, 0)


def plain_kernel(rows_ref, count_ref, coef_ref, x_ref, right_ref, out_ref, packed_ref, weight_ref, many_ref):
    partition(rows_ref, count_ref, coef_ref, packed_ref, weight_ref, many_ref)
    out_ref[...] = jnp.zeros_like(out_ref)
    add_plain(many_ref[0], x_ref, right_ref, packed_ref, weight_ref, out_ref)


def left_kernel(packed_ref, weight_ref, many_ref, x_ref, right_ref, left_ref, before_ref, out_ref):
    out_ref[...] = before_ref[...]
    add_left(many_ref[1], x_ref, right_ref, left_ref, packed_ref, weight_ref, out_ref)


def both_kernel(packed_ref, weight_ref, many_ref, x_ref, right_ref, left_ref, image_ref, search_ref, *rest):
    out_ref, image_out_ref, search_out_ref, sems = rest
    copies = (
        pltpu.make_async_copy(image_ref, image_out_ref, sems.at[0]),
        pltpu.make_async_copy(search_ref, search_out_ref, sems.at[1]),
    )
    for copy in copies:
        copy.start()
    out_ref[...] = jnp.zeros_like(out_ref)
    add_plain(many_ref[0], x_ref, right_ref, packed_ref, weight_ref, out_ref)
    add_left(many_ref[1], x_ref, right_ref, left_ref, packed_ref, weight_ref, out_ref)
    for copy in copies:
        copy.wait()


def copy_to(src, dst, send_sem, recv_sem, device):
    return pltpu.make_async_remote_copy(
        src_ref=src,
        dst_ref=dst,
        send_sem=send_sem,
        recv_sem=recv_sem,
        device_id={"sec": device},
        device_id_type=pl.DeviceIdType.MESH,
    )


def greet_all(me, n):
    barrier = pltpu.get_barrier_semaphore()
    for s in range(1, n):
        pl.semaphore_signal(
            barrier, inc=1, device_id={"sec": (me + s) % n}, device_id_type=pl.DeviceIdType.MESH
        )
    pl.semaphore_wait(barrier, n - 1)


def gather(me, n, whole, sends, recvs, make_part):
    half = n // 2
    rows = whole.shape[1] // PARTS
    side, major = me % 2, me // 2
    partner = me + 1 - 2 * side
    rises, falls = major < half - 1, major > 0

    def piece(b, c, way, to):
        ref = whole.at[b, pl.ds(c * rows, rows)]
        return copy_to(ref, ref, sends.at[way, b, c], recvs.at[b, c], to)

    def up(b, c):
        return piece(b, c, 0, (me + 2) % n)

    def down(b, c):
        return piece(b, c, 1, (me + n - 2) % n)

    def across(b, c):
        return piece(b, c, 2, partner)

    def when(ok, action):
        pl.when(ok)(action)

    def reached(d):
        return ((up, rises, major - d, major >= d), (down, falls, major + d, major + d < half))

    for c in range(PARTS):
        make_part(pl.ds(c * rows, rows))
        across(me, c).start()
        when(rises, lambda: up(me, c).start())
        when(falls, lambda: down(me, c).start())
    for d in range(1, half):
        for c in range(PARTS):
            for onward, more, m, ok in reached(d):

                def take(c=c, onward=onward, more=more, b=2 * m + side):
                    across(b, c).wait_recv()
                    when(more, lambda: onward(b, c).start())
                    across(b, c).start()

                when(ok, take)
    for c in range(PARTS):
        across(partner, c).wait_recv()
    for d in range(1, half):
        for c in range(PARTS):
            for _, _, m, ok in reached(d):
                when(ok, lambda: across(2 * m + 1 - side, c).wait_recv())
    for c in range(PARTS):
        across(me, c).wait_send()
        when(rises, lambda: up(me, c).wait_send())
        when(falls, lambda: down(me, c).wait_send())
    for d in range(1, half):
        for c in range(PARTS):
            for onward, more, m, ok in reached(d):

                def settle(c=c, onward=onward, more=more, b=2 * m + side):
                    when(more, lambda: onward(b, c).wait_send())
                    across(b, c).wait_send()

                when(ok, settle)


def coded(value, code_ref, scale_ref):
    groups = value.reshape(value.shape[0] // 8, 8, value.shape[1])
    top = jnp.maximum(jnp.max(jnp.abs(groups), axis=0), 1e-30)
    scale_ref[...] = top * (1.0 / LEVELS)
    steps = jnp.round(groups * (LEVELS / top)[None])
    code_ref[...] = steps.reshape(value.shape).astype(jnp.int32).astype(jnp.int16)


def decoded(code_ref, scale_ref):
    code = code_ref[...].astype(jnp.int32).astype(jnp.float32)
    groups = code.reshape(code.shape[0] // 8, 8, code.shape[1]) * scale_ref[...][None]
    return groups.reshape(code.shape)


def reduce_copies(me, n, bufs):
    partner = me + 1 - 2 * (me % 2)
    (y_code, y_scale, y_code_in, y_scale_in, z_code, z_scale, z_code_in, z_scale_in, sems) = bufs

    def y_copies(t):
        return (
            copy_to(y_code.at[t], y_code_in.at[t], sems.at[0, t], sems.at[1, t], partner),
            copy_to(y_scale.at[t], y_scale_in.at[t], sems.at[2, t], sems.at[3, t], partner),
        )

    def z_copies(t):
        to = (me + 2 * (t // CUTS)) % n
        return (
            copy_to(z_code.at[t], z_code_in.at[t], sems.at[4, t], sems.at[5, t], to),
            copy_to(z_scale.at[t], z_scale_in.at[t], sems.at[6, t], sems.at[7, t], to),
        )

    return y_copies, z_copies


def reduce_scatter(me, n, partial, image, bufs, meanwhile=None):
    slots = n // 2 * CUTS
    rows = partial.shape[1] // CUTS
    partner = me + 1 - 2 * (me % 2)
    (y_code, y_scale, y_code_in, y_scale_in, z_code, z_scale, z_code_in, z_scale_in, sems) = bufs
    y_copies, z_copies = reduce_copies(me, n, bufs)

    def cut(t):
        return pl.ds(pl.multiple_of((t % CUTS) * rows, rows), rows)

    def send_y(i, carry):
        t = (i + CUTS) % slots
        coded(partial[(partner + 2 * (t // CUTS)) % n, cut(t)], y_code.at[t], y_scale.at[t])
        for copy in y_copies(t):
            copy.start()
        return carry

    lax.fori_loop(0, slots, send_y, 0)
    if meanwhile is not None:
        meanwhile()

    def send_z(t, carry):
        for copy in y_copies(t):
            copy.wait_recv()
        added = partial[(me + 2 * (t // CUTS)) % n, cut(t)] + decoded(y_code_in.at[t], y_scale_in.at[t])
        coded(added, z_code.at[t], z_scale.at[t])
        for copy in z_copies(t):
            copy.start()
        return carry

    lax.fori_loop(CUTS, slots, send_z, 0)

    def own(t, carry):
        for copy in y_copies(t):
            copy.wait_recv()
        image[0, cut(t)] = partial[me, cut(t)] + decoded(y_code_in.at[t], y_scale_in.at[t])
        return carry

    lax.fori_loop(0, CUTS, own, 0)

    def take_z(t, carry):
        for copy in z_copies(t):
            copy.wait_recv()
        image[0, cut(t)] += decoded(z_code_in.at[t], z_scale_in.at[t])
        return carry

    lax.fori_loop(CUTS, slots, take_z, 0)


def reduce_scatter_drain(me, n, bufs):
    slots = n // 2 * CUTS
    y_copies, z_copies = reduce_copies(me, n, bufs)

    def settle_y(t, carry):
        for copy in y_copies(t):
            copy.wait_send()
        return carry

    def settle_z(t, carry):
        for copy in z_copies(t):
            copy.wait_send()
        return carry

    lax.fori_loop(0, slots, settle_y, 0)
    lax.fori_loop(CUTS, slots, settle_z, 0)


def reduce_scratch(n, dim):
    slots = n // 2 * CUTS
    pair = [VM((slots, dim // CUTS, dim), jnp.int16), VM((slots, 8, dim), jnp.float32)]
    return pair * 4 + [pltpu.SemaphoreType.DMA((8, slots))]


def total(value):
    return jnp.sum(jnp.sum(value, axis=0, keepdims=True), axis=1, keepdims=True)


def gather_kernel(n, mine_ref, right_ref, whole_ref, right_near_ref, loaded, sends, recvs):
    me = lax.axis_index("sec")
    load = pltpu.make_async_copy(mine_ref.at[0], whole_ref.at[me], loaded.at[0])
    bring = pltpu.make_async_copy(right_ref, right_near_ref, loaded.at[1])
    load.start()
    bring.start()
    greet_all(me, n)
    load.wait()
    gather(me, n, whole_ref, sends, recvs, lambda rows: None)
    bring.wait()


def step_kernel(n, partial_ref, wave_ref, energy_ref, image_ref, search_ref, whole_ref, *rest):
    inverse_ref, scaled_ref, residual_ref, sums_ref, *bufs, sum_sems, sends, recvs = rest
    dim = wave_ref.shape[1]
    me = lax.axis_index("sec")
    greet_all(me, n)
    row = lax.broadcasted_iota(jnp.int32, (8, 128), 0)

    def wave_sums():
        wave = wave_ref[0].astype(jnp.float32)
        down = lax.broadcasted_iota(jnp.int32, (dim, dim), 0)
        along = lax.broadcasted_iota(jnp.int32, (dim, dim), 1)
        diagonal = jnp.where(down == along, energy_ref[me, 0:1, :], 0.0)
        energy = jnp.sum(diagonal, axis=1, keepdims=True) + energy_ref[me, 1:2, :]
        inverse = 1.0 / energy
        wr = wave * inverse
        inverse_ref[...] = inverse
        scaled_ref[...] = wr
        tile = jnp.zeros((8, 128), jnp.float32)
        for i, value in ((0, total(wave * wave)), (2, total(wave * wr)), (3, total(wr * wr))):
            tile = jnp.where(row == i, value, tile)
        sums_ref[me] = tile

    reduce_scatter(me, n, partial_ref, image_ref, bufs, wave_sums)

    wave = wave_ref[0].astype(jnp.float32)
    xx = sums_ref[me, 0:1, 0:1]
    safe = jnp.where(xx > 0, xx, 1.0)
    xh = total(wave * image_ref[0])
    theta_here = xh / safe
    c = image_ref[0] * inverse_ref[...] - theta_here * scaled_ref[...]
    residual_ref[...] = c
    s = total(wave * c)
    alpha_here = s / safe
    v = residual_ref[...] - alpha_here * wave_ref[0].astype(jnp.float32)
    p = total(v * v)
    q = total(v * scaled_ref[...])
    left_over = total(v * wave_ref[0].astype(jnp.float32))
    tile = sums_ref[me]
    for i, value in ((1, xh), (4, s), (5, p), (6, q), (7, left_over)):
        tile = jnp.where(row == i, value, tile)
    sums_ref[me] = tile

    def sums_copy(slot, to, block):
        return copy_to(sums_ref.at[block], sums_ref.at[block], sum_sems.at[0, slot], sum_sems.at[1, slot], to)

    for slot in range(1, n):
        sums_copy(slot, (me + slot) % n, me).start()
    for slot in range(1, n):
        sums_copy(slot, (me + slot) % n, (me + n - slot) % n).wait_recv()
    xx_k, xh_k, b_k, r_k, s_k, p_k, q_k, l_k = (sums_ref[:, i, :] for i in range(8))
    safe_k = jnp.where(xx_k > 0, xx_k, 1.0)
    xx_all = jnp.sum(xx_k, axis=0, keepdims=True)
    theta = jnp.sum(xh_k, axis=0, keepdims=True) / xx_all
    d_theta = theta - xh_k / safe_k
    alpha = jnp.sum(s_k - d_theta * b_k, axis=0, keepdims=True) / xx_all
    d_alpha = alpha - s_k / safe_k
    tt_k = (
        p_k
        + d_theta * d_theta * r_k
        + d_alpha * d_alpha * xx_k
        - 2.0 * d_theta * q_k
        - 2.0 * d_alpha * l_k
        + 2.0 * d_theta * d_alpha * b_k
    )
    tt = jnp.maximum(jnp.sum(tt_k, axis=0, keepdims=True), 0.0)
    cells = n * dim * dim
    factor = (1.0 / jnp.sqrt(tt / cells + 1e-06))[:, :1]
    theta, alpha = theta[:, :1], alpha[:, :1]

    def find(rows):
        part = wave_ref[0, rows].astype(jnp.float32)
        orth = (image_ref[0, rows] - theta * part) * inverse_ref[rows] - alpha * part
        found = (orth * factor).astype(jnp.bfloat16)
        search_ref[0, rows] = found
        whole_ref[me, rows] = found

    gather(me, n, whole_ref, sends, recvs, find)
    for slot in range(1, n):
        sums_copy(slot, (me + slot) % n, me).wait_send()
    reduce_scatter_drain(me, n, bufs)


def reduce_kernel(n, partial_ref, image_ref, *bufs):
    me = lax.axis_index("sec")
    greet_all(me, n)
    reduce_scatter(me, n, partial_ref, image_ref, bufs)
    reduce_scatter_drain(me, n, bufs)


def vmem(k):
    return [pl.BlockSpec(memory_space=VM)] * k


def smem(k):
    return [pl.BlockSpec(memory_space=SM)] * k


def params(blocks, collective_id=None):
    size = (4 << 20) + (blocks << 18)
    if collective_id is None:
        return pltpu.CompilerParams(vmem_limit_bytes=size)
    return pltpu.CompilerParams(vmem_limit_bytes=size, collective_id=collective_id, has_side_effects=True)


def body(n, wave, diag_energy, term_list, term_count, term_coef, edge_env, right_env):
    mine = wave[0]
    dim = mine.shape[1]
    energy = diag_energy[0]
    left_env = shifted(edge_env, "seg", 1)[0]
    right_here = right_env[0]
    terms = term_list.shape[1]
    cap = (terms + STEP + 127) // 128 * 128
    dma = pltpu.SemaphoreType.DMA
    blocks_bf = jax.ShapeDtypeStruct((n, dim, dim), jnp.bfloat16)
    blocks_f = jax.ShapeDtypeStruct((n, dim, dim), jnp.float32)
    one_f = jax.ShapeDtypeStruct((1, dim, dim), jnp.float32)
    one_bf = jax.ShapeDtypeStruct((1, dim, dim), jnp.bfloat16)
    lists = (
        jax.ShapeDtypeStruct((2 * cap,), jnp.int32),
        jax.ShapeDtypeStruct((2 * cap,), jnp.float32),
        jax.ShapeDtypeStruct((2,), jnp.int32),
    )

    envs = 2 * right_here.shape[0]
    gather_sems = [dma((3, n, PARTS)), dma((n, PARTS))]
    hbm = pl.BlockSpec(memory_space=pltpu.HBM)
    anywhere = pl.BlockSpec(memory_space=pl.ANY)
    gathered, right_near = pl.pallas_call(
        functools.partial(gather_kernel, n),
        out_shape=(blocks_bf, jax.ShapeDtypeStruct(right_here.shape, right_here.dtype)),
        in_specs=[hbm, hbm],
        out_specs=tuple(vmem(2)),
        scratch_shapes=[dma((2,))] + gather_sems,
        compiler_params=params(n + envs, 0),
    )(mine, right_here)
    cost = pl.CostEstimate(flops=terms * dim**3, bytes_accessed=8 << 20, transcendentals=0)
    first, packed, weight, many = pl.pallas_call(
        plain_kernel,
        out_shape=(blocks_f, *lists),
        in_specs=smem(3) + vmem(2),
        out_specs=(*vmem(1), *smem(3)),
        compiler_params=params(3 * n + envs),
        cost_estimate=cost,
    )(term_list[0].T, term_count, term_coef, gathered, right_near)
    partial_first = pl.pallas_call(
        left_kernel,
        out_shape=blocks_f,
        in_specs=smem(3) + vmem(4),
        out_specs=vmem(1)[0],
        compiler_params=params(3 * n + envs),
        cost_estimate=cost,
    )(packed, weight, many, gathered, right_near, left_env, first)
    image_first, search_mine, search_whole = pl.pallas_call(
        functools.partial(step_kernel, n),
        out_shape=(one_f, one_bf, blocks_bf),
        in_specs=vmem(3),
        out_specs=tuple(vmem(3)),
        scratch_shapes=[VM((dim, dim), jnp.float32)] * 3
        + [VM((n, 8, 128), jnp.float32)]
        + reduce_scratch(n, dim)
        + [dma((2, n))]
        + gather_sems,
        compiler_params=params(4 * n, 1),
    )(partial_first, mine, energy)
    partial_second, image_out, search_out = pl.pallas_call(
        both_kernel,
        out_shape=(blocks_f, one_f, one_bf),
        in_specs=smem(3) + vmem(3) + [anywhere] * 2,
        out_specs=(*vmem(1), hbm, hbm),
        scratch_shapes=[dma((2,))],
        compiler_params=params(3 * n + envs),
        cost_estimate=cost,
    )(packed, weight, many, search_whole, right_near, left_env, image_first, search_mine)
    image_second = pl.pallas_call(
        functools.partial(reduce_kernel, n),
        out_shape=one_f,
        in_specs=vmem(1),
        out_specs=vmem(1)[0],
        scratch_shapes=reduce_scratch(n, dim),
        compiler_params=params(3 * n, 2),
    )(partial_second)
    return (image_out[None], search_out[None], image_second[None])


def solution(mesh):
    return jax.shard_map(
        functools.partial(body, mesh.shape["sec"]),
        mesh=mesh,
        in_specs=(
            P("seg", "sec", None, None),
            P("seg", None, None, None),
            P("seg", "sec", None),
            P("seg", "sec"),
            P("seg", "sec"),
            P("seg", "sec", None, None),
            P("seg", "sec", None, None),
        ),
        out_specs=(
            P("seg", "sec", None, None),
            P("seg", "sec", None, None),
            P("seg", "sec", None, None),
        ),
        check_vma=False,
    )
```

profile of v0, /device:TPU:0, one launch (start us, length us, event | category | flops | bytes accessed | tf_op | source)
XLA Modules:
  0.0 107.8 jit_solution(10977623348734598877)
XLA Ops:
  0.6 0.0 copy-start.5
  0.6 0.0 copy-start.4
  0.7 2.6 %collective-permute-start = (bf16[1,16,256,256]{3,2,1,0:T(8,128)(2,1)}, bf16[1,16,256,256]{3,2,1,0:T(8,128)(2,1)S(1)}, u32[]{:S(2)}, u32[]{:S(2)}) collective-permute-start(bf16[1,16,256,256]{3,2,1,0:T(8,128)(2,1)} %param.12), channel_id=1, source_target_pairs={{0,8},{8,16},{16,24},{1,9},{9,17},{17,25},{2,10},{10,18},{18,26},{... | collective-permute-start | bytes 6291464 | tf_op jit(solution)/shard_map/ppermute | solution.py:21
  3.9 0.0 copy-start
  3.9 1.6 %copy-done = bf16[1,16,256,256]{3,2,1,0:T(8,128)(2,1)S(1)} copy-done((bf16[1,16,256,256]{3,2,1,0:T(8,128)(2,1)S(1)}, bf16[1,16,256,256]{3,2,1,0:T(8,128)(2,1)}, u32[]{:S(2)}) %copy-start) | copy-done | bytes 2097176
  5.5 0.0 copy-start.1
  5.5 0.9 copy-done.1
  6.4 20.5 %shard_map.94 = (bf16[8,256,256]{2,1,0:T(8,128)(2,1)S(1)}, bf16[16,256,256]{2,1,0:T(8,128)(2,1)S(1)}) custom-call(bf16[1,256,256]{2,1,0:T(8,128)(2,1)S(1)} %bitcast.14, bf16[16,256,256]{2,1,0:T(8,128)(2,1)S(1)} %bitcast.10), custom_call_target="tpu_custom_call" | custom-call | tf_op jit(solution)/shard_map/pallas_call | solution.py:443
  26.9 0.0 copy-done.5
  27.0 0.0 copy-done.4
  27.0 3.0 %shard_map.95 = (f32[8,256,256]{2,1,0:T(8,128)S(1)}, s32[256]{0:T(256)S(1)}, f32[256]{0:T(256)S(1)}, s32[2]{0:T(128)S(1)}) custom-call(s32[4,96]{1,0:T(4,128)S(1)} %bitcast.17, s32[1,1]{1,0:T(1,128)S(6)} %copy.11.count_ref, f32[1,96]{1,0:T(1,128)S(1)} %copy-done.5, bf16[8,256,256]{2,1,0:T(8,128)(2,1)S(1)} %get-tuple-element.15.x_ref, ...), custom_call_target="tpu_custom_call" | custom-call | flops 1610612736 | bytes 8388608 | tf_op jit(solution)/shard_map/pallas_call | solution.py:452
  30.0 0.0 collective-permute-done
  30.0 0.0 copy-start.2
  30.0 0.0 copy-start.3
  30.0 1.8 %shard_map.96.partial_ref = f32[8,256,256]{2,1,0:T(8,128)S(1)} custom-call(s32[256]{0:T(256)S(1)} %get-tuple-element.17.packed_ref, f32[256]{0:T(256)S(1)} %get-tuple-element.18.weight_ref, s32[2]{0:T(128)S(1)} %get-tuple-element.19.many_ref, bf16[8,256,256]{2,1,0:T(8,128)(2,1)S(1)} %get-tuple-element.15.x_ref, ...), custom_call_target="tpu_custom_call" | custom-call | flops 1610612736 | bytes 8388608 | tf_op jit(solution)/shard_map/pallas_call | solution.py:460
  31.8 0.0 copy-done.2
  31.8 0.0 copy-done.3
  31.8 48.3 %shard_map.97 = (f32[1,256,256]{2,1,0:T(8,128)S(1)}, bf16[1,256,256]{2,1,0:T(8,128)(2,1)S(1)}, bf16[8,256,256]{2,1,0:T(8,128)(2,1)S(1)}) custom-call(f32[8,256,256]{2,1,0:T(8,128)S(1)} %shard_map.96.partial_ref, bf16[1,256,256]{2,1,0:T(8,128)(2,1)S(1)} %bitcast.15, f32[8,2,256]{2,1,0:T(2,128)S(1)} %bitcast.16), custom_call_target="tpu_custom_call" | custom-call | tf_op jit(solution)/shard_map/pallas_call | solution.py:468
  80.2 3.2 %shard_map.98 = (f32[8,256,256]{2,1,0:T(8,128)S(1)}, f32[1,256,256]{2,1,0:T(8,128)}, bf16[1,256,256]{2,1,0:T(8,128)(2,1)}) custom-call(s32[256]{0:T(256)S(1)} %get-tuple-element.17.packed_ref, f32[256]{0:T(256)S(1)} %get-tuple-element.18.weight_ref, s32[2]{0:T(128)S(1)} %get-tuple-element.19.many_ref, bf16[8,256,256]{2,1,0:T(8,128)(2,1)S(1)} %get-tuple-element.21.x_ref, ...), custom_call_target="tpu_custom_call" | custom-call | flops 1610612736 | bytes 8388608 | tf_op jit(solution)/shard_map/pallas_call | solution.py:480
  83.4 23.7 %shard_map.99 = f32[1,256,256]{2,1,0:T(8,128)S(1)} custom-call(f32[8,256,256]{2,1,0:T(8,128)S(1)} %get-tuple-element.26.partial_ref), custom_call_target="tpu_custom_call" | custom-call | tf_op jit(solution)/shard_map/pallas_call | solution.py:489
  107.1 0.7 copy.12
Async XLA Ops:
  0.6 26.3 %copy-start.5 = (f32[1,96]{1,0:T(1,128)S(1)}, f32[1,96]{1,0:T(1,128)}, u32[]{:S(2)}) copy-start(f32[1,96]{1,0:T(1,128)} %coef_ref.1) | copy-start | bytes 1156
  0.6 26.3 %copy-start.4 = (s32[1,96,4]{1,2,0:T(4,128)S(1)}, s32[1,96,4]{1,2,0:T(4,128)}, u32[]{:S(2)}) copy-start(s32[1,96,4]{1,2,0:T(4,128)} %param.9) | copy-start | bytes 4612
  0.7 29.3 %collective-permute-start = (bf16[1,16,256,256]{3,2,1,0:T(8,128)(2,1)}, bf16[1,16,256,256]{3,2,1,0:T(8,128)(2,1)S(1)}, u32[]{:S(2)}, u32[]{:S(2)}) collective-permute-start(bf16[1,16,256,256]{3,2,1,0:T(8,128)(2,1)} %param.12), channel_id=1, source_target_pairs={{0,8},{8,16},{16,24},{1,9},{9,17},{17,25},{2,10},{10,18},{18,26},{... | collective-permute-start | bytes 6291464 | tf_op jit(solution)/shard_map/ppermute | solution.py:21
  3.9 1.6 %copy-start = (bf16[1,16,256,256]{3,2,1,0:T(8,128)(2,1)S(1)}, bf16[1,16,256,256]{3,2,1,0:T(8,128)(2,1)}, u32[]{:S(2)}) copy-start(bf16[1,16,256,256]{3,2,1,0:T(8,128)(2,1)} %param.13) | copy-start | bytes 6291460
  5.5 0.9 copy-start.1
  30.0 1.8 %copy-start.2 = (bf16[1,1,256,256]{3,2,1,0:T(8,128)(2,1)S(1)}, bf16[1,1,256,256]{3,2,1,0:T(8,128)(2,1)}, u32[]{:S(2)}) copy-start(bf16[1,1,256,256]{3,2,1,0:T(8,128)(2,1)} %param.7) | copy-start | bytes 393220
  30.0 1.8 %copy-start.3 = (f32[1,8,2,256]{3,2,1,0:T(2,128)S(1)}, f32[1,8,2,256]{3,2,1,0:T(2,128)}, u32[]{:S(2)}) copy-start(f32[1,8,2,256]{3,2,1,0:T(2,128)} %param.8) | copy-start | bytes 49156
where the time goes:
time: 109 us; the launch traced here: 108 us
  Pallas kernels  101 us (93%)
  local copies, waits for them, and re-layouts  3.21 us (3%)
  starting transfers between devices  2.62 us (2%)
  between operations  1.41 us (1%)
    pallas_call x1, Pallas kernels, body(): pl.pallas_call(functools.partial(step_kernel, n), out_shape=(one_f, one_b...  48.3 us
    pallas_call x1, Pallas kernels, body(): pl.pallas_call(functools.partial(reduce_kernel, n), out_shape=one_f, in_s...  23.7 us
    pallas_call x1, Pallas kernels, body(): pl.pallas_call(functools.partial(gather_kernel, n), out_shape=(blocks_bf,...  20.5 us
    unnamed x13, local copies, waits for them, and re-layouts  3.21 us
    pallas_call x1, Pallas kernels, body(): pl.pallas_call(both_kernel, out_shape=(blocks_f, one_f, one_bf), in_specs...  3.17 us
    pallas_call x1, Pallas kernels, body(): pl.pallas_call(plain_kernel, out_shape=(blocks_f, *lists), in_specs=smem(...  2.99 us
    ppermute x1, starting transfers between devices, shifted(): return lax.ppermute(value, axis, pairs)  2.62 us
  transfers between devices with their start and end apart: 1, of which 0 were waited for; matrix products, arithmetic and copies ran while one was open for 0% of the time, Pallas kernels for 22%

commit v1 on v0

--- a/solution.py
+++ b/solution.py
@@ -7,7 +7,7 @@
 from jax.experimental.pallas import tpu as pltpu
 from jax.sharding import PartitionSpec as P
 
-STEP = 4
+STEP = 8
 PARTS = 4
 CUTS = 2
 LEVELS = 32767.0
@@ -46,51 +46,49 @@
     return code % 256, (code // 256) % 256, code // 65536
 
 
-def add_plain(many, x_ref, right_ref, packed_ref, weight_ref, out_ref):
-    def advance(turn, carry):
-        done = []
+def add_step(plain, left, turn, x_ref, right_ref, left_ref, packed_ref, weight_ref, out_ref):
+    cap = packed_ref.shape[0] // 2
+    rounded, done = [], []
+    if left:
+        for u in range(STEP):
+            at = cap + turn * STEP + u
+            src, tgt, chan = fields(packed_ref, at)
+            product = jnp.dot(x_ref[src], right_ref[chan], preferred_element_type=jnp.float32)
+            rounded.append((tgt, chan, weight_ref[at], product.astype(jnp.bfloat16)))
+    if plain:
         for u in range(STEP):
             at = turn * STEP + u
             src, tgt, chan = fields(packed_ref, at)
             product = jnp.dot(x_ref[src], right_ref[chan], preferred_element_type=jnp.float32)
             done.append((tgt, weight_ref[at], product))
-        for tgt, weight, product in done:
-            out_ref[tgt] += weight * product
-        return carry
-
-    lax.fori_loop(0, (many + STEP - 1) // STEP, advance, 0)
-
-
-def add_left(many, x_ref, right_ref, left_ref, packed_ref, weight_ref, out_ref):
-    cap = packed_ref.shape[0] // 2
-
+    for tgt, chan, weight, value in rounded:
+        leftward = jnp.dot(left_ref[chan], value, preferred_element_type=jnp.float32)
+        done.append((tgt, weight, leftward))
+    for tgt, weight, value in done:
+        out_ref[tgt] += weight * value
+
+
+def add_terms(first, last, plain, left, *refs):
     def advance(turn, carry):
-        rounded = []
-        for u in range(STEP):
-            at = cap + turn * STEP + u
-            src, tgt, chan = fields(packed_ref, at)
-            product = jnp.dot(x_ref[src], right_ref[chan], preferred_element_type=jnp.float32)
-            rounded.append((at, tgt, chan, product.astype(jnp.bfloat16)))
-        done = []
-        for at, tgt, chan, value in rounded:
-            leftward = jnp.dot(left_ref[chan], value, preferred_element_type=jnp.float32)
-            done.append((tgt, weight_ref[at], leftward))
-        for tgt, weight, leftward in done:
-            out_ref[tgt] += weight * leftward
-        return carry
-
-    lax.fori_loop(0, (many + STEP - 1) // STEP, advance, 0)
+        add_step(plain, left, turn, *refs)
+        return carry
+
+    lax.fori_loop(first, last, advance, 0)
+
+
+def steps(many):
+    return (many + STEP - 1) // STEP
 
 
 def plain_kernel(rows_ref, count_ref, coef_ref, x_ref, right_ref, out_ref, packed_ref, weight_ref, many_ref):
     partition(rows_ref, count_ref, coef_ref, packed_ref, weight_ref, many_ref)
     out_ref[...] = jnp.zeros_like(out_ref)
-    add_plain(many_ref[0], x_ref, right_ref, packed_ref, weight_ref, out_ref)
+    add_terms(0, steps(many_ref[0]), True, False, x_ref, right_ref, None, packed_ref, weight_ref, out_ref)
 
 
 def left_kernel(packed_ref, weight_ref, many_ref, x_ref, right_ref, left_ref, before_ref, out_ref):
     out_ref[...] = before_ref[...]
-    add_left(many_ref[1], x_ref, right_ref, left_ref, packed_ref, weight_ref, out_ref)
+    add_terms(0, steps(many_ref[1]), False, True, x_ref, right_ref, left_ref, packed_ref, weight_ref, out_ref)
 
 
 def both_kernel(packed_ref, weight_ref, many_ref, x_ref, right_ref, left_ref, image_ref, search_ref, *rest):
@@ -102,8 +100,12 @@
     for copy in copies:
         copy.start()
     out_ref[...] = jnp.zeros_like(out_ref)
-    add_plain(many_ref[0], x_ref, right_ref, packed_ref, weight_ref, out_ref)
-    add_left(many_ref[1], x_ref, right_ref, left_ref, packed_ref, weight_ref, out_ref)
+    refs = (x_ref, right_ref, left_ref, packed_ref, weight_ref, out_ref)
+    n0, n1 = steps(many_ref[0]), steps(many_ref[1])
+    common = jnp.minimum(n0, n1)
+    add_terms(0, common, True, True, *refs)
+    add_terms(common, n0, True, False, *refs)
+    add_terms(common, n1, False, True, *refs)
     for copy in copies:
         copy.wait()
 

time: 109 us -> 102 us (0.936); the launches traced: 108 us -> 104 us
  Pallas kernels: 101 us -> 96.6 us
    pallas_call x1, Pallas kernels: 23.7 us -> 18.9 us  [body(): pl.pallas_call(functools.partial(reduce_kernel, n), out_shape=one_f, in_s...]
    pallas_call x1, Pallas kernels: 48.3 us -> 43.7 us  [body(): pl.pallas_call(functools.partial(step_kernel, n), out_shape=(one_f, one_b...]
    pallas_call x1, Pallas kernels: 3.17 us -> 5.44 us  [body(): pl.pallas_call(both_kernel, out_shape=(blocks_f, one_f, one_bf), in_specs...]
    pallas_call x1, Pallas kernels: 1.8 us -> 3.88 us  [body(): pl.pallas_call(left_kernel, out_shape=blocks_f, in_specs=smem(3) + vmem(4...]
    pallas_call x1, Pallas kernels: 2.99 us -> 4.17 us  [body(): pl.pallas_call(plain_kernel, out_shape=(blocks_f, *lists), in_specs=smem(...]
  transfers between devices with their start and end apart: 1 -> 1, of which waited for: 0 -> 0; matrix products, arithmetic and copies ran while one was open for 0% -> 0% of each run, Pallas kernels for 22% -> 24%
where the time goes in v1:
time: 102 us; the launch traced here: 104 us
  Pallas kernels  96.6 us (95%)
  local copies, waits for them, and re-layouts  3.21 us (3%)
  starting transfers between devices  2.62 us (3%)
  between operations  1.41 us (1%)
    pallas_call x1, Pallas kernels, body(): pl.pallas_call(functools.partial(step_kernel, n), out_shape=(one_f, one_b...  43.7 us
    pallas_call x1, Pallas kernels, body(): pl.pallas_call(functools.partial(gather_kernel, n), out_shape=(blocks_bf,...  20.5 us
    pallas_call x1, Pallas kernels, body(): pl.pallas_call(functools.partial(reduce_kernel, n), out_shape=one_f, in_s...  18.9 us
    pallas_call x1, Pallas kernels, body(): pl.pallas_call(both_kernel, out_shape=(blocks_f, one_f, one_bf), in_specs...  5.44 us
    pallas_call x1, Pallas kernels, body(): pl.pallas_call(plain_kernel, out_shape=(blocks_f, *lists), in_specs=smem(...  4.17 us
    pallas_call x1, Pallas kernels, body(): pl.pallas_call(left_kernel, out_shape=blocks_f, in_specs=smem(3) + vmem(4...  3.88 us
    unnamed x13, local copies, waits for them, and re-layouts  3.21 us
    ppermute x1, starting transfers between devices, shifted(): return lax.ppermute(value, axis, pairs)  2.62 us
  transfers between devices with their start and end apart: 1, of which 0 were waited for; matrix products, arithmetic and copies ran while one was open for 0% of the time, Pallas kernels for 24%

profile of v1, /device:TPU:0, one launch (start us, length us, event | category | flops | bytes accessed | tf_op | source)
XLA Modules:
  0.0 103.8 jit_solution(9718466819977897614)
XLA Ops:
  0.6 0.0 copy-start.5
  0.6 0.0 copy-start.4
  0.7 2.6 %collective-permute-start = (bf16[1,16,256,256]{3,2,1,0:T(8,128)(2,1)}, bf16[1,16,256,256]{3,2,1,0:T(8,128)(2,1)S(1)}, u32[]{:S(2)}, u32[]{:S(2)}) collective-permute-start(bf16[1,16,256,256]{3,2,1,0:T(8,128)(2,1)} %param.12), channel_id=1, source_target_pairs={{0,8},{8,16},{16,24},{1,9},{9,17},{17,25},{2,10},{10,18},{18,26},{... | collective-permute-start | bytes 6291464 | tf_op jit(solution)/shard_map/ppermute | solution.py:21
  3.9 0.0 copy-start
  3.9 1.6 %copy-done = bf16[1,16,256,256]{3,2,1,0:T(8,128)(2,1)S(1)} copy-done((bf16[1,16,256,256]{3,2,1,0:T(8,128)(2,1)S(1)}, bf16[1,16,256,256]{3,2,1,0:T(8,128)(2,1)}, u32[]{:S(2)}) %copy-start) | copy-done | bytes 2097176
  5.5 0.0 copy-start.1
  5.5 0.9 copy-done.1
  6.4 20.5 %shard_map.94 = (bf16[8,256,256]{2,1,0:T(8,128)(2,1)S(1)}, bf16[16,256,256]{2,1,0:T(8,128)(2,1)S(1)}) custom-call(bf16[1,256,256]{2,1,0:T(8,128)(2,1)S(1)} %bitcast.14, bf16[16,256,256]{2,1,0:T(8,128)(2,1)S(1)} %bitcast.10), custom_call_target="tpu_custom_call" | custom-call | tf_op jit(solution)/shard_map/pallas_call | solution.py:445
  26.9 0.0 copy-done.5
  27.0 0.0 copy-done.4
  27.0 4.2 %shard_map.95 = (f32[8,256,256]{2,1,0:T(8,128)S(1)}, s32[256]{0:T(256)S(1)}, f32[256]{0:T(256)S(1)}, s32[2]{0:T(128)S(1)}) custom-call(s32[4,96]{1,0:T(4,128)S(1)} %bitcast.17, s32[1,1]{1,0:T(1,128)S(6)} %copy.11.count_ref, f32[1,96]{1,0:T(1,128)S(1)} %copy-done.5, bf16[8,256,256]{2,1,0:T(8,128)(2,1)S(1)} %get-tuple-element.15.x_ref, ...), custom_call_target="tpu_custom_call" | custom-call | flops 1610612736 | bytes 8388608 | tf_op jit(solution)/shard_map/pallas_call | solution.py:454
  31.1 0.0 collective-permute-done
  31.1 0.0 copy-start.2
  31.2 0.0 copy-start.3
  31.2 3.9 %shard_map.96.partial_ref = f32[8,256,256]{2,1,0:T(8,128)S(1)} custom-call(s32[256]{0:T(256)S(1)} %get-tuple-element.17.packed_ref, f32[256]{0:T(256)S(1)} %get-tuple-element.18.weight_ref, s32[2]{0:T(128)S(1)} %get-tuple-element.19.many_ref, bf16[8,256,256]{2,1,0:T(8,128)(2,1)S(1)} %get-tuple-element.15.x_ref, ...), custom_call_target="tpu_custom_call" | custom-call | flops 1610612736 | bytes 8388608 | tf_op jit(solution)/shard_map/pallas_call | solution.py:462
  35.1 0.0 copy-done.2
  35.1 0.0 copy-done.3
  35.1 43.7 %shard_map.97 = (f32[1,256,256]{2,1,0:T(8,128)S(1)}, bf16[1,256,256]{2,1,0:T(8,128)(2,1)S(1)}, bf16[8,256,256]{2,1,0:T(8,128)(2,1)S(1)}) custom-call(f32[8,256,256]{2,1,0:T(8,128)S(1)} %shard_map.96.partial_ref, bf16[1,256,256]{2,1,0:T(8,128)(2,1)S(1)} %bitcast.15, f32[8,2,256]{2,1,0:T(2,128)S(1)} %bitcast.16), custom_call_target="tpu_custom_call" | custom-call | tf_op jit(solution)/shard_map/pallas_call | solution.py:470
  78.8 5.4 %shard_map.98 = (f32[8,256,256]{2,1,0:T(8,128)S(1)}, f32[1,256,256]{2,1,0:T(8,128)}, bf16[1,256,256]{2,1,0:T(8,128)(2,1)}) custom-call(s32[256]{0:T(256)S(1)} %get-tuple-element.17.packed_ref, f32[256]{0:T(256)S(1)} %get-tuple-element.18.weight_ref, s32[2]{0:T(128)S(1)} %get-tuple-element.19.many_ref, bf16[8,256,256]{2,1,0:T(8,128)(2,1)S(1)} %get-tuple-element.21.x_ref, ...), custom_call_target="tpu_custom_call" | custom-call | flops 1610612736 | bytes 8388608 | tf_op jit(solution)/shard_map/pallas_call | solution.py:482
  84.2 18.9 %shard_map.99 = f32[1,256,256]{2,1,0:T(8,128)S(1)} custom-call(f32[8,256,256]{2,1,0:T(8,128)S(1)} %get-tuple-element.26.partial_ref), custom_call_target="tpu_custom_call" | custom-call | tf_op jit(solution)/shard_map/pallas_call | solution.py:491
  103.1 0.7 copy.12
Async XLA Ops:
  0.6 26.3 %copy-start.5 = (f32[1,96]{1,0:T(1,128)S(1)}, f32[1,96]{1,0:T(1,128)}, u32[]{:S(2)}) copy-start(f32[1,96]{1,0:T(1,128)} %coef_ref.1) | copy-start | bytes 1156
  0.6 26.3 %copy-start.4 = (s32[1,96,4]{1,2,0:T(4,128)S(1)}, s32[1,96,4]{1,2,0:T(4,128)}, u32[]{:S(2)}) copy-start(s32[1,96,4]{1,2,0:T(4,128)} %param.9) | copy-start | bytes 4612
  0.7 30.5 %collective-permute-start = (bf16[1,16,256,256]{3,2,1,0:T(8,128)(2,1)}, bf16[1,16,256,256]{3,2,1,0:T(8,128)(2,1)S(1)}, u32[]{:S(2)}, u32[]{:S(2)}) collective-permute-start(bf16[1,16,256,256]{3,2,1,0:T(8,128)(2,1)} %param.12), channel_id=1, source_target_pairs={{0,8},{8,16},{16,24},{1,9},{9,17},{17,25},{2,10},{10,18},{18,26},{... | collective-permute-start | bytes 6291464 | tf_op jit(solution)/shard_map/ppermute | solution.py:21
  3.9 1.6 %copy-start = (bf16[1,16,256,256]{3,2,1,0:T(8,128)(2,1)S(1)}, bf16[1,16,256,256]{3,2,1,0:T(8,128)(2,1)}, u32[]{:S(2)}) copy-start(bf16[1,16,256,256]{3,2,1,0:T(8,128)(2,1)} %param.13) | copy-start | bytes 6291460
  5.5 0.9 copy-start.1
  31.1 3.9 %copy-start.2 = (bf16[1,1,256,256]{3,2,1,0:T(8,128)(2,1)S(1)}, bf16[1,1,256,256]{3,2,1,0:T(8,128)(2,1)}, u32[]{:S(2)}) copy-start(bf16[1,1,256,256]{3,2,1,0:T(8,128)(2,1)} %param.7) | copy-start | bytes 393220
  31.2 3.9 %copy-start.3 = (f32[1,8,2,256]{3,2,1,0:T(2,128)S(1)}, f32[1,8,2,256]{3,2,1,0:T(2,128)}, u32[]{:S(2)}) copy-start(f32[1,8,2,256]{3,2,1,0:T(2,128)} %param.8) | copy-start | bytes 49156
